TPU v7x, 32 devices: a whole 2x2x4 slice. The times are simulated.
32 devices in a mesh: dp: 4 (over y, core), row: 2 (over x), col: 4 (over z).
Axes of the slice: x: 2, y: 2, z: 4, core: 2. Of those that a mesh axis runs over, the one named last changes fastest.
Arguments:
- tokens: bfloat16 [1024, 6144], P(('dp', 'col'), 'row'), may hold values from -6 to 6
- cotangent: bfloat16 [1024, 6144], P(('dp', 'col'), 'row'), may hold values from -6 to 6
- pre_act: bfloat16 [1024, 12288], P('dp', 'col'), may hold values from -6 to 6
- weight_in: bfloat16 [6144, 12288], P('row', 'col'), may hold values from -0.078125 to 0.078125
- weight_out: bfloat16 [12288, 6144], P('col', 'row'), may hold values from -0.0546875 to 0.0546875
Outputs:
- grad_tokens: bfloat16 [1024, 6144], P(('dp', 'col'), 'row')
- grad_in: float32 [6144, 12288], P('row', ('col', 'dp'))
- grad_out: float32 [12288, 6144], P(('col', 'dp'), 'row')
All inputs are finite; a program needn't handle non-finite values.
Results may differ from a plain program's by a relative error of at most 0.023.
Values may be sent and summed in bfloat16 or wider, within the bound.
A program may use at most 192 MiB of HBM per device.

v0:
```python
import jax
import jax.numpy as jnp
from jax import lax
from jax.sharding import PartitionSpec as P


def gelu_value(a):
    return 0.5 * a * (1.0 + lax.erf(a * 0.7071067811865476))


def gelu_slope(a):
    return (
        0.5 * (1.0 + lax.erf(a * 0.7071067811865476))
        + a * jnp.exp(-0.5 * a * a) * 0.3989422804014327
    )


def shards(tokens, cotangent, pre_act, weight_in, weight_out):
    contract = (((1,), (1,)), ((), ()))
    lead = (((0,), (0,)), ((), ()))
    tok_all, cot_all = (
        lax.all_gather(tokens, "col", axis=0, tiled=True),
        lax.all_gather(cotangent, "col", axis=0, tiled=True),
    )
    replica = tok_all.shape[0]
    total_tokens = replica * lax.axis_size("dp")
    factor = float(total_tokens) ** (-0.5)
    pre_float = pre_act.astype(jnp.float32)
    summed = lax.psum(
        lax.dot_general(cot_all, weight_out, contract, preferred_element_type=jnp.float32).astype(
            jnp.bfloat16
        ),
        "row",
    ).astype(jnp.float32)
    grad_pre = (summed * gelu_slope(pre_float)).astype(jnp.bfloat16)
    grad_tokens = lax.psum_scatter(
        lax.dot_general(grad_pre, weight_in, contract, preferred_element_type=jnp.float32).astype(
            jnp.bfloat16
        ),
        "col",
        scatter_dimension=0,
        tiled=True,
    )
    hidden = gelu_value(pre_float).astype(jnp.bfloat16)
    first = lax.dot_general(tok_all, grad_pre, lead, preferred_element_type=jnp.float32) * factor
    second = lax.dot_general(hidden, cot_all, lead, preferred_element_type=jnp.float32) * factor
    grad_in, grad_out = (
        lax.psum_scatter(first.astype(jnp.bfloat16), "dp", scatter_dimension=1, tiled=True).astype(
            jnp.float32
        ),
        lax.psum_scatter(second.astype(jnp.bfloat16), "dp", scatter_dimension=0, tiled=True).astype(
            jnp.float32
        ),
    )
    return (grad_tokens, grad_in, grad_out)


def solution(mesh):
    in_specs = (
        P(("dp", "col"), "row"),
        P(("dp", "col"), "row"),
        P("dp", "col"),
        P("row", "col"),
        P("col", "row"),
    )
    out_specs = (P(("dp", "col"), "row"), P("row", ("col", "dp")), P(("col", "dp"), "row"))
    return jax.shard_map(shards, mesh=mesh, in_specs=in_specs, out_specs=out_specs, check_vma=False)
```

profile of v0, /device:TPU:0, one launch (start us, length us, event | category | flops | bytes accessed | tf_op | source)
XLA Modules:
  0.0 469.2 jit_solution(8932405080684482068)
XLA Ops:
  7.2 0.0 all-gather.3.cloned.1.call-start
  7.2 0.7 all-gather.3.cloned.1.call-update
  7.9 0.0 all-gather.5.cloned.1.call-start
  7.9 0.7 all-gather.5.cloned.1.call-update
  8.6 0.0 copy-start
  8.7 0.0 all-reduce.2.cloned.1.call-start
  8.7 40.7 %all-gather.3.cloned.1.call-done = bf16[256,3072]{1,0:T(8,128)(2,1)} async-done(((bf16[64,3072]{1,0:T(8,128)(2,1)}), bf16[256,3072]{1,0:T(8,128)(2,1)}) %all-gather.3.cloned.1.call-update) | async-done | bytes 1572880 | tf_op jit(solution)/shard_map/all_gather | solution.py:23
  49.4 0.0 copy-start.2
  49.4 12.7 %convolution_convert_fusion.1 = bf16[256,3072]{1,0:T(8,128)(2,1)} fusion(bf16[256,3072]{1,0:T(8,128)(2,1)} %all-gather.3.cloned.1.call-done, bf16[3072,3072]{1,0:T(8,128)(2,1)} %param.9), kind=kOutput, calls=%fused_computation.9 | convolution fusion | flops 4832624640 | bytes 22020096 | tf_op jit(solution)/shard_map/dot_general | solution.py:30
  62.1 0.0 all-reduce.2.cloned.1.call-update
  62.1 0.0 reduce-scatter.8.cloned.1.call-start
  62.1 0.0 copy-done
  62.1 0.0 copy-done.2
  62.2 9.3 %multiply_convert_fusion = bf16[3072,3072]{1,0:T(8,128)(2,1)} fusion(bf16[256,3072]{1,0:T(8,128)(2,1)S(1)} %copy-done.2, bf16[256,3072]{1,0:T(8,128)(2,1)S(1)} %copy-done), kind=kOutput, calls=%fused_computation | convolution fusion | flops 4855431168 | bytes 22020096 | tf_op jit(solution)/shard_map/dot_general | solution.py:46
  71.5 0.0 reduce-scatter.8.cloned.1.call-update
  71.5 0.0 reduce-scatter.6.cloned.1.call-start
  71.5 15.4 %all-gather.5.cloned.1.call-done = bf16[256,3072]{1,0:T(8,128)(2,1)} async-done(((bf16[64,3072]{1,0:T(8,128)(2,1)}), bf16[256,3072]{1,0:T(8,128)(2,1)}) %all-gather.5.cloned.1.call-update) | async-done | bytes 1572880 | tf_op jit(solution)/shard_map/all_gather | solution.py:22
  86.9 53.3 %all-reduce.2.cloned.1.call-done = bf16[256,3072]{1,0:T(8,128)(2,1)} async-done(((bf16[256,3072]{1,0:T(8,128)(2,1)}), bf16[256,3072]{1,0:T(8,128)(2,1)}) %all-reduce.2.cloned.1.call-update) | async-done | bytes 1572880 | tf_op jit(solution)/shard_map/psum | solution.py:29
  140.2 13.6 %fusion = bf16[3072,3072]{0,1:T(8,128)(2,1)} fusion(bf16[256,3072]{1,0:T(8,128)(2,1)} %all-gather.5.cloned.1.call-done, bf16[256,3072]{1,0:T(8,128)(2,1)S(1)} %copy-done, bf16[256,3072]{1,0:T(8,128)(2,1)} %all-reduce.2.cloned.1.call-done), kind=kOutput, calls=%fused_computation.2 | convolution fusion | flops 4860149760 | bytes 23592960 | tf_op jit(solution)/shard_map/dot_general | solution.py:45
  153.8 0.0 copy-start.1
  153.8 0.0 reduce-scatter.6.cloned.1.call-update
  153.8 0.0 reduce-scatter.4.cloned.1.call-start
  153.9 1.8 copy-done.1
  155.7 14.6 %convolution_convert_fusion = bf16[256,3072]{1,0:T(8,128)(2,1)} fusion(bf16[3072,3072]{1,0:T(8,128)(2,1)} %param.8, bf16[256,3072]{1,0:T(8,128)(2,1)S(1)} %copy-done, bf16[256,3072]{1,0:T(8,128)(2,1)S(1)} %copy-done.1), kind=kOutput, calls=%fused_computation.8 | convolution fusion | flops 4842061824 | bytes 23592960 | tf_op jit(solution)/shard_map/dot_general | solution.py:37
  170.3 0.0 reduce-scatter.4.cloned.1.call-update
  170.3 112.0 %reduce-scatter.8.cloned.1.call-done = bf16[768,3072]{1,0:T(8,128)(2,1)} async-done(((bf16[3072,3072]{1,0:T(8,128)(2,1)}), bf16[768,3072]{1,0:T(8,128)(2,1)}) %reduce-scatter.8.cloned.1.call-update) | async-done | bytes 4718608 | tf_op jit(solution)/shard_map/reduce_scatter | solution.py:51
  282.2 7.4 %convert_element_type.43 = f32[768,3072]{1,0:T(8,128)} convert(bf16[768,3072]{1,0:T(8,128)(2,1)} %reduce-scatter.8.cloned.1.call-done) | non-fusion elementwise | flops 2359296 | bytes 14155776 | tf_op jit(solution)/shard_map/convert_element_type | solution.py:51
  289.6 134.6 %reduce-scatter.6.cloned.1.call-done = bf16[3072,768]{0,1:T(8,128)(2,1)} async-done(((bf16[3072,3072]{0,1:T(8,128)(2,1)}), bf16[3072,768]{0,1:T(8,128)(2,1)}) %reduce-scatter.6.cloned.1.call-update) | async-done | bytes 4718608 | tf_op jit(solution)/shard_map/reduce_scatter | solution.py:48
  424.2 7.4 %copy.8 = f32[3072,768]{1,0:T(8,128)} copy(bf16[3072,768]{0,1:T(8,128)(2,1)} %reduce-scatter.6.cloned.1.call-done) | data formatting | bytes 14155776
  431.6 30.8 %reduce-scatter.4.cloned.1.call-done = bf16[64,3072]{1,0:T(8,128)(2,1)} async-done(((bf16[256,3072]{1,0:T(8,128)(2,1)}), bf16[64,3072]{1,0:T(8,128)(2,1)}) %reduce-scatter.4.cloned.1.call-update) | async-done | bytes 393232 | tf_op jit(solution)/shard_map/reduce_scatter | solution.py:36
Async XLA Ops:
  7.2 42.2 %all-gather.3.cloned.1.call-start = ((), (), s32[]{:S(2)}) async-start(), calls=%async_computation.3 | async-start | bytes 1966080 | tf_op jit(solution)/shard_map/all_gather | solution.py:23
  7.9 79.1 %all-gather.5.cloned.1.call-start = ((), (), s32[]{:S(2)}) async-start(), calls=%async_computation.6 | async-start | bytes 1966080 | tf_op jit(solution)/shard_map/all_gather | solution.py:22
  8.6 53.5 %copy-start = (bf16[256,3072]{1,0:T(8,128)(2,1)S(1)}, bf16[256,3072]{1,0:T(8,128)(2,1)}, u32[]{:S(2)}) copy-start(bf16[256,3072]{1,0:T(8,128)(2,1)} %param.7) | copy-start | bytes 4718596
  8.7 131.5 %all-reduce.2.cloned.1.call-start = ((), (), s32[]{:S(2)}) async-start(), calls=%async_computation.4 | async-start | bytes 3145728 | tf_op jit(solution)/shard_map/psum | solution.py:29
  49.4 12.8 %copy-start.2 = (bf16[256,3072]{1,0:T(8,128)(2,1)S(1)}, bf16[256,3072]{1,0:T(8,128)(2,1)}, u32[]{:S(2)}) copy-start(bf16[256,3072]{1,0:T(8,128)(2,1)} %all-gather.3.cloned.1.call-done) | copy-start | bytes 4718596
  62.1 220.2 %reduce-scatter.8.cloned.1.call-start = ((), (), s32[]{:S(2)}) async-start(), calls=%async_computation.8 | async-start | bytes 23592960 | tf_op jit(solution)/shard_map/reduce_scatter | solution.py:51
  71.5 352.7 %reduce-scatter.6.cloned.1.call-start = ((), (), s32[]{:S(2)}) async-start(), calls=%async_computation.7 | async-start | bytes 23592960 | tf_op jit(solution)/shard_map/reduce_scatter | solution.py:48
  153.8 1.9 copy-start.1
  153.8 308.5 %reduce-scatter.4.cloned.1.call-start = ((), (), s32[]{:S(2)}) async-start(), calls=%async_computation.5 | async-start | bytes 1966080 | tf_op jit(solution)/shard_map/reduce_scatter | solution.py:36
Sparse Core Ops, SparseCore 0:
  9.6 39.7 all-gather.2
  51.0 35.9 all-gather.4
  89.8 50.3 all-reduce.1
  142.8 139.3 reduce-scatter.7
  284.7 139.4 reduce-scatter.5
  427.0 35.2 reduce-scatter.3
where the time goes:
time: 470 us; the launch traced here: 469 us
  waiting for transfers between devices  388 us (83%)
  matrix products  50.2 us (11%)
  between operations  14.1 us (3%)
  local copies, waits for them, and re-layouts  9.18 us (2%)
  other arithmetic  7.37 us (2%)
    reduce_scatter x1, waiting for transfers between devices, shards(): lax.psum_scatter(first.astype(jnp.bfloat16), 'dp', scatter_dimension=1, t...  135 us
    reduce_scatter x1, waiting for transfers between devices, shards(): lax.psum_scatter(second.astype(jnp.bfloat16), 'dp', scatter_dimension=0,...  112 us
    psum x1, waiting for transfers between devices, shards(): lax.psum(lax.dot_general(cot_all, weight_out, contract, preferred_element...  53.3 us
    all_gather x1, waiting for transfers between devices, shards(): lax.all_gather(cotangent, 'col', axis=0, tiled=True)  40.7 us
    reduce_scatter x1, waiting for transfers between devices, shards(): lax.psum_scatter(lax.dot_general(grad_pre, weight_in, contract, preferred...  30.8 us
    all_gather x1, waiting for transfers between devices, shards(): lax.all_gather(tokens, 'col', axis=0, tiled=True)  15.4 us
    dot_general x1, matrix products, shards(): lax.dot_general(grad_pre, weight_in, contract, preferred_element_type=jnp...  14.6 us
    dot_general x1, matrix products, shards(): lax.dot_general(tok_all, grad_pre, lead, preferred_element_type=jnp.float32)  13.6 us
  transfers between devices with their start and end apart: 6, of which 6 were waited for; matrix products, arithmetic and copies ran while one was open for 14% of the time, Pallas kernels for 0%

commit v1 on v0

--- a/solution.py
+++ b/solution.py
@@ -26,11 +26,14 @@
     total_tokens = replica * lax.axis_size("dp")
     factor = float(total_tokens) ** (-0.5)
     pre_float = pre_act.astype(jnp.float32)
-    summed = lax.psum(
-        lax.dot_general(cot_all, weight_out, contract, preferred_element_type=jnp.float32).astype(
-            jnp.bfloat16
+    summed = jnp.sum(
+        lax.all_gather(
+            lax.dot_general(
+                cot_all, weight_out, contract, preferred_element_type=jnp.float32
+            ).astype(jnp.bfloat16),
+            "row",
         ),
-        "row",
+        axis=0,
     ).astype(jnp.float32)
     grad_pre = (summed * gelu_slope(pre_float)).astype(jnp.bfloat16)
     grad_tokens = lax.psum_scatter(

time: 470 us -> 473 us (level)
    psum x1 -> x0, waiting for transfers between devices: 53.3 us -> none  [shards(): lax.psum(lax.dot_general(cot_all, weight_out, contract, preferred_element...]
    all_gather x0 -> x1, waiting for transfers between devices: none -> 32.7 us  [shards(): lax.all_gather(lax.dot_general(cot_all, weight_out, contract, preferred_e...]
    all_gather x1, waiting for transfers between devices: 15.4 us -> 36 us  [shards(): lax.all_gather(tokens, 'col', axis=0, tiled=True)]
  transfers between devices with their start and end apart: 6 -> 6, of which waited for: 6 -> 6; matrix products, arithmetic and copies ran while one was open for 14% -> 12% of each run, Pallas kernels for 0% -> 0%
where the time goes in v1:
time: 473 us
  waiting for transfers between devices  389 us (82%)
  matrix products  51.9 us (11%)
  between operations  14.1 us (3%)
  other arithmetic  10 us (2%)
  local copies, waits for them, and re-layouts  7.4 us (2%)
    reduce_scatter x1, waiting for transfers between devices, shards(): lax.psum_scatter(first.astype(jnp.bfloat16), 'dp', scatter_dimension=1, t...  135 us
    reduce_scatter x1, waiting for transfers between devices, shards(): lax.psum_scatter(second.astype(jnp.bfloat16), 'dp', scatter_dimension=0,...  112 us
    all_gather x1, waiting for transfers between devices, shards(): lax.all_gather(cotangent, 'col', axis=0, tiled=True)  41.4 us
    all_gather x1, waiting for transfers between devices, shards(): lax.all_gather(tokens, 'col', axis=0, tiled=True)  36 us
    all_gather x1, waiting for transfers between devices, shards(): lax.all_gather(lax.dot_general(cot_all, weight_out, contract, preferred_e...  32.7 us
    reduce_scatter x1, waiting for transfers between devices, shards(): lax.psum_scatter(lax.dot_general(grad_pre, weight_in, contract, preferred...  30.7 us
    dot_general x1, matrix products, shards(): lax.dot_general(grad_pre, weight_in, contract, preferred_element_type=jnp...  14.6 us
    dot_general x1, matrix products, shards(): lax.dot_general(tok_all, grad_pre, lead, preferred_element_type=jnp.float32)  14.3 us
  transfers between devices with their start and end apart: 6, of which 6 were waited for; matrix products, arithmetic and copies ran while one was open for 12% of the time, Pallas kernels for 0%

profile of v1, /device:TPU:0, one launch (start us, length us, event | category | flops | bytes accessed | tf_op | source)
XLA Modules:
  0.0 472.6 jit_solution(906536459708538113)
XLA Ops:
  7.2 0.0 all-gather.5.cloned.1.call-start
  7.2 0.7 all-gather.5.cloned.1.call-update
  7.9 0.0 copy-start
  7.9 0.0 all-gather.9.cloned.1.call-start
  8.0 41.4 %all-gather.5.cloned.1.call-done = bf16[256,3072]{1,0:T(8,128)(2,1)} async-done(((bf16[64,3072]{1,0:T(8,128)(2,1)}), bf16[256,3072]{1,0:T(8,128)(2,1)}) %all-gather.5.cloned.1.call-update) | async-done | bytes 1572880 | tf_op jit(solution)/shard_map/all_gather | solution.py:23
  49.4 0.0 copy-start.1
  49.4 12.7 %convolution_convert_fusion.1 = bf16[256,3072]{1,0:T(8,128)(2,1)} fusion(bf16[256,3072]{1,0:T(8,128)(2,1)} %all-gather.5.cloned.1.call-done, bf16[3072,3072]{1,0:T(8,128)(2,1)} %param.9), kind=kOutput, calls=%fused_computation.9 | convolution fusion | flops 4832624640 | bytes 22020096 | tf_op jit(solution)/shard_map/dot_general | solution.py:31
  62.1 0.0 all-gather.9.cloned.1.call-update
  62.1 0.0 all-gather.7.cloned.1.call-start
  62.1 0.7 all-gather.7.cloned.1.call-update
  62.8 0.0 reduce-scatter.8.cloned.1.call-start
  62.9 0.0 copy-done
  62.9 0.0 copy-done.1
  62.9 10.3 %multiply_convert_fusion = bf16[3072,3072]{1,0:T(8,128)(2,1)} fusion(bf16[256,3072]{1,0:T(8,128)(2,1)S(1)} %copy-done.1, bf16[256,3072]{1,0:T(8,128)(2,1)S(1)} %copy-done), kind=kOutput, calls=%fused_computation | convolution fusion | flops 4855431168 | bytes 22020096 | tf_op jit(solution)/shard_map/dot_general | solution.py:49
  73.2 0.0 reduce-scatter.8.cloned.1.call-update
  73.3 0.0 reduce-scatter.6.cloned.1.call-start
  73.3 32.7 %all-gather.9.cloned.1.call-done = bf16[512,3072]{1,0:T(8,128)(2,1)} async-done(((bf16[256,3072]{1,0:T(8,128)(2,1)}), bf16[512,3072]{1,0:T(8,128)(2,1)}) %all-gather.9.cloned.1.call-update) | async-done | bytes 3145744 | tf_op jit(solution)/shard_map/all_gather | solution.py:30
  106.0 2.7 reduce_sum.12
  108.7 36.0 %all-gather.7.cloned.1.call-done = bf16[256,3072]{1,0:T(8,128)(2,1)} async-done(((bf16[64,3072]{1,0:T(8,128)(2,1)}), bf16[256,3072]{1,0:T(8,128)(2,1)}) %all-gather.7.cloned.1.call-update) | async-done | bytes 1572880 | tf_op jit(solution)/shard_map/all_gather | solution.py:22
  144.8 14.3 %fusion = bf16[3072,3072]{0,1:T(8,128)(2,1)} fusion(bf16[256,3072]{1,0:T(8,128)(2,1)} %all-gather.7.cloned.1.call-done, bf16[256,3072]{1,0:T(8,128)(2,1)S(1)} %copy-done, bf16[256,3072]{1,0:T(8,128)(2,1)S(1)} %reduce_sum.12), kind=kOutput, calls=%fused_computation.2 | convolution fusion | flops 4860149760 | bytes 23592960 | tf_op jit(solution)/shard_map/dot_general | solution.py:48
  159.0 0.0 reduce-scatter.6.cloned.1.call-update
  159.1 0.2 reduce-scatter.4.cloned.1.call-start
  159.3 14.6 %convolution_convert_fusion = bf16[256,3072]{1,0:T(8,128)(2,1)} fusion(bf16[3072,3072]{1,0:T(8,128)(2,1)} %param.8, bf16[256,3072]{1,0:T(8,128)(2,1)S(1)} %copy-done, bf16[256,3072]{1,0:T(8,128)(2,1)S(1)} %reduce_sum.12), kind=kOutput, calls=%fused_computation.8 | convolution fusion | flops 4842061824 | bytes 23592960 | tf_op jit(solution)/shard_map/dot_general | solution.py:40
  173.9 0.0 reduce-scatter.4.cloned.1.call-update
  173.9 111.6 %reduce-scatter.8.cloned.1.call-done = bf16[768,3072]{1,0:T(8,128)(2,1)} async-done(((bf16[3072,3072]{1,0:T(8,128)(2,1)}), bf16[768,3072]{1,0:T(8,128)(2,1)}) %reduce-scatter.8.cloned.1.call-update) | async-done | bytes 4718608 | tf_op jit(solution)/shard_map/reduce_scatter | solution.py:54
  285.6 7.4 %convert_element_type.45 = f32[768,3072]{1,0:T(8,128)} convert(bf16[768,3072]{1,0:T(8,128)(2,1)} %reduce-scatter.8.cloned.1.call-done) | non-fusion elementwise | flops 2359296 | bytes 14155776 | tf_op jit(solution)/shard_map/convert_element_type | solution.py:54
  292.9 134.8 %reduce-scatter.6.cloned.1.call-done = bf16[3072,768]{0,1:T(8,128)(2,1)} async-done(((bf16[3072,3072]{0,1:T(8,128)(2,1)}), bf16[3072,768]{0,1:T(8,128)(2,1)}) %reduce-scatter.6.cloned.1.call-update) | async-done | bytes 4718608 | tf_op jit(solution)/shard_map/reduce_scatter | solution.py:51
  427.7 7.4 %copy.8 = f32[3072,768]{1,0:T(8,128)} copy(bf16[3072,768]{0,1:T(8,128)(2,1)} %reduce-scatter.6.cloned.1.call-done) | data formatting | bytes 14155776
  435.1 30.7 %reduce-scatter.4.cloned.1.call-done = bf16[64,3072]{1,0:T(8,128)(2,1)} async-done(((bf16[256,3072]{1,0:T(8,128)(2,1)}), bf16[64,3072]{1,0:T(8,128)(2,1)}) %reduce-scatter.4.cloned.1.call-update) | async-done | bytes 393232 | tf_op jit(solution)/shard_map/reduce_scatter | solution.py:39
Async XLA Ops:
  7.2 42.2 %all-gather.5.cloned.1.call-start = ((), (), s32[]{:S(2)}) async-start(), calls=%async_computation.3 | async-start | bytes 1966080 | tf_op jit(solution)/shard_map/all_gather | solution.py:23
  7.9 55.0 %copy-start = (bf16[256,3072]{1,0:T(8,128)(2,1)S(1)}, bf16[256,3072]{1,0:T(8,128)(2,1)}, u32[]{:S(2)}) copy-start(bf16[256,3072]{1,0:T(8,128)(2,1)} %param.7) | copy-start | bytes 4718596
  7.9 98.1 %all-gather.9.cloned.1.call-start = ((), (), s32[]{:S(2)}) async-start(), calls=%async_computation.8 | async-start | bytes 4718592 | tf_op jit(solution)/shard_map/all_gather | solution.py:30
  49.4 13.5 %copy-start.1 = (bf16[256,3072]{1,0:T(8,128)(2,1)S(1)}, bf16[256,3072]{1,0:T(8,128)(2,1)}, u32[]{:S(2)}) copy-start(bf16[256,3072]{1,0:T(8,128)(2,1)} %all-gather.5.cloned.1.call-done) | copy-start | bytes 4718596
  62.1 82.7 %all-gather.7.cloned.1.call-start = ((), (), s32[]{:S(2)}) async-start(), calls=%async_computation.5 | async-start | bytes 1966080 | tf_op jit(solution)/shard_map/all_gather | solution.py:22
  62.8 222.7 %reduce-scatter.8.cloned.1.call-start = ((), (), s32[]{:S(2)}) async-start(), calls=%async_computation.7 | async-start | bytes 23592960 | tf_op jit(solution)/shard_map/reduce_scatter | solution.py:54
  73.3 354.5 %reduce-scatter.6.cloned.1.call-start = ((), (), s32[]{:S(2)}) async-start(), calls=%async_computation.6 | async-start | bytes 23592960 | tf_op jit(solution)/shard_map/reduce_scatter | solution.py:51
  159.1 306.7 %reduce-scatter.4.cloned.1.call-start = ((), (), s32[]{:S(2)}) async-start(), calls=%async_computation.4 | async-start | bytes 1966080 | tf_op jit(solution)/shard_map/reduce_scatter | solution.py:39
Sparse Core Ops, SparseCore 0:
  9.6 39.7 all-gather.4
  62.2 43.7 all-gather.8
  107.6 37.0 all-gather.6
  147.2 138.3 reduce-scatter.7
  288.2 139.4 reduce-scatter.5
  430.4 35.2 reduce-scatter.3
